TPU v7x, 32 devices: a whole 2x2x4 slice. The times are simulated.
32 devices in a mesh: band: 16 (over z, y, core), col: 2 (over x).
Axes of the slice: x: 2, y: 2, z: 4, core: 2. Of those that a mesh axis runs over, the one named last changes fastest.
Arguments:
- valence: bfloat16 [8, 64, 64, 128], P('col'), may hold values from -6 to 6
- conduction: bfloat16 [64, 64, 64, 128], P('band'), may hold values from -6 to 6
- energy_valence: float32 [8], P('col'), may hold values from -6 to -1
- energy_conduction: float32 [64], P('band'), may hold values from 0.5 to 6
- occ_valence: int32 [8], P('col'), may hold values from 1 to 2
- occ_conduction: int32 [64], P('band'), may hold values from 0 to 1
- gvec_index: int32 [10240], replicated, may hold values from 0 to 262143, as said below
Outputs:
- chi_zero: float32 [2, 10240, 10240], P(None, 'band', 'col')
Inputs may be any that keep to these rules, and one draw needn't show every extreme that they name: `gvec_index`: distinct indices of the 10240 grid points with the shortest wave vectors, where index x * 64 * 64 + y * 64 + z stands for the vector with components ((x + 32) mod 64) - 32 and so on; ordered by length, equal lengths in any order.
All inputs are finite; a program needn't handle non-finite values.
Results may differ from a plain program's by a relative error of at most 0.01.
Values may be sent and summed in bfloat16 or wider, within the bound.
A program may use at most 320 MiB of HBM per device.

v0:
```python
import math

import jax
import jax.numpy as jnp
from jax import lax
from jax.sharding import PartitionSpec as P

NG = 64


def dft_parts(grid):
    freq = jnp.arange(grid, dtype=jnp.int32)
    product = freq[:, None] * freq[None, :] % grid
    angle = 2.0 * math.pi / grid * product.astype(jnp.float32)
    cosine = jnp.cos(angle) / math.sqrt(grid)
    sine = jnp.sin(angle) / math.sqrt(grid)
    return (cosine, sine)


def swap_parts(field, grid):
    return jnp.concatenate([field[..., grid:], -field[..., :grid]], axis=-1)


def along_middle(field, pair_table, form, grid):
    stacked = jnp.stack([field, swap_parts(field, grid)], axis=1)
    return jnp.einsum(form, pair_table, stacked, preferred_element_type=jnp.float32).astype(
        jnp.bfloat16
    )


def contract(rows_part, block):
    imag_cols = jnp.stack([-block[:, :, 1], block[:, :, 0]], axis=2)
    dims = (((0, 1, 2), (0, 1, 2)), ((), ()))
    real_tile = lax.dot_general(rows_part, block, dims, preferred_element_type=jnp.float32)
    imag_tile = lax.dot_general(rows_part, imag_cols, dims, preferred_element_type=jnp.float32)
    return jnp.stack([real_tile, imag_tile], axis=0)


def local(
    valence, conduction, energy_valence, energy_conduction, occ_valence, occ_conduction, gvec_index
):
    cosine, sine = dft_parts(NG)
    pair_table = jnp.stack([cosine, sine]).astype(jnp.bfloat16)
    full_table = jnp.stack([jnp.stack([cosine, sine]), jnp.stack([-sine, cosine])]).astype(
        jnp.bfloat16
    )
    z_matrix = jnp.transpose(full_table, (1, 3, 0, 2)).reshape(2 * NG, 2 * NG)
    val_local = valence.shape[0]
    cond_local = conduction.shape[0]
    val_re = valence[..., :NG][:, None].astype(jnp.float32)
    val_im = valence[..., NG:][:, None].astype(jnp.float32)
    cond_re = conduction[..., :NG][None].astype(jnp.float32)
    cond_im = conduction[..., NG:][None].astype(jnp.float32)
    real_part = val_re * cond_re + val_im * cond_im
    imag_part = val_re * cond_im - val_im * cond_re
    field = jnp.concatenate([real_part, imag_part], axis=-1).astype(jnp.bfloat16)
    field = field.reshape(val_local * cond_local, NG, NG, 2 * NG)
    field = along_middle(field, pair_table, "ikx,bixym->bkym", NG)
    field = along_middle(field, pair_table, "iky,bixym->bxkm", NG)
    field = jnp.einsum("bxym,mn->bxyn", field, z_matrix, preferred_element_type=jnp.float32).astype(
        jnp.bfloat16
    )
    flat = field.reshape(val_local, cond_local, NG * NG * 2 * NG)
    z_pos = gvec_index % NG
    base_pos = (gvec_index - z_pos) * 2 + z_pos
    rho = jnp.stack(
        [jnp.take(flat, base_pos, axis=2), jnp.take(flat, base_pos + NG, axis=2)], axis=2
    )
    total_val = val_local * lax.axis_size("col")
    total_cond = cond_local * lax.axis_size("band")
    occ_diff = (occ_valence[:, None] - occ_conduction[None, :]).astype(jnp.float32)
    weight = (
        occ_diff
        / (energy_valence[:, None] - energy_conduction[None, :])
        / math.sqrt(total_val * total_cond)
    )
    weighted = (weight[:, :, None, None] * rho.astype(jnp.float32)).astype(jnp.bfloat16)
    row_block = lax.all_to_all(weighted, "band", split_axis=3, concat_axis=1, tiled=True)
    rows_all = lax.all_gather(row_block, "col", axis=0, tiled=True)
    all_cond = lax.all_gather(rho, "band", axis=1, tiled=True)
    col_block = lax.all_to_all(all_cond, "col", split_axis=3, concat_axis=0, tiled=True)
    tile = contract(rows_all, col_block)
    return tile


def solution(mesh):
    return jax.shard_map(
        local,
        mesh=mesh,
        in_specs=(
            P("col", None, None, None),
            P("band", None, None, None),
            P("col"),
            P("band"),
            P("col"),
            P("band"),
            P(),
        ),
        out_specs=P(None, "band", "col"),
        check_vma=False,
    )
```

profile of v0, /device:TPU:0, one launch (start us, length us, event | category | flops | bytes accessed | tf_op | source)
XLA Modules:
  0.0 993.1 jit_solution(8391618559558381797)
XLA Ops:
  7.4 0.0 all-gather.5.cloned.1.call-start
  7.4 11.3 %slice_convert_fusion.3 = (f32[4,64,64,64]{3,2,1,0:T(8,128)}, f32[4,64,64,64]{3,2,1,0:T(8,128)}) fusion(bf16[4,64,64,128]{3,2,1,0:T(8,128)(2,1)} %param.9), kind=kLoop, calls=%fused_computation.32 | loop fusion | flops 2097152 | bytes 12582912 | tf_op jit(solution)/shard_map/convert_element_type | solution.py:50
  18.7 11.5 %copy.21 = f32[4,64,64,64]{3,1,2,0:T(8,128)} copy(f32[4,64,64,64]{3,2,1,0:T(8,128)} %get-tuple-element.14) | data formatting | bytes 8388608 | tf_op jit(solution)/shard_map/convert_element_type | solution.py:50
  30.2 0.0 copy-done.1
  30.2 7.8 slice_convert_fusion.2
  37.9 8.4 copy.22
  46.4 0.0 copy-start
  46.4 0.0 slice-start
  46.4 14.5 %copy.23 = f32[4,64,64,64]{3,1,2,0:T(8,128)} copy(f32[4,64,64,64]{3,2,1,0:T(8,128)} %get-tuple-element.15) | data formatting | bytes 8388608 | tf_op jit(solution)/shard_map/convert_element_type | solution.py:51
  60.9 12.0 %copy.24 = f32[4,64,64,64]{3,1,2,0:T(8,128)} copy(f32[4,64,64,64]{3,2,1,0:T(8,128)} %get-tuple-element.17) | data formatting | bytes 8388608 | tf_op jit(solution)/shard_map/convert_element_type | solution.py:53
  72.9 0.0 copy-done
  72.9 0.0 slice-done
  72.9 0.0 slice-done.1
  73.0 15.2 %subtract_convert_fusion = bf16[4,4,64,64,64]{4,2,3,1,0:T(8,128)(2,1)} fusion(f32[4,64,64,64]{3,1,2,0:T(8,128)} %copy.24, f32[4,64,64,64]{3,1,2,0:T(8,128)} %copy.23, f32[4,64,64,64]{3,1,2,0:T(8,128)S(1)} %copy.22, f32[4,64,64,64]{3,1,2,0:T(8,128)S(1)} %bitcast.89), kind=kLoop, calls=%fused_computation.13 | loop fusion | flops 16777216 | bytes 25165824 | tf_op jit(solution)/shard_map/convert.12
  88.2 25.8 %fusion.46 = (bf16[4,4,64,64,64]{4,2,3,1,0:T(8,128)(2,1)}, bf16[4,4,64,64,64]{4,2,3,1,0:T(8,128)(2,1)}) fusion(f32[4,64,64,64]{3,1,2,0:T(8,128)} %copy.24, f32[4,64,64,64]{3,1,2,0:T(8,128)} %copy.23, f32[4,64,64,64]{3,1,2,0:T(8,128)} %copy-done, f32[4,64,64,64]{3,1,2,0:T(8,128)} %copy.21), kind=kLoop, calls=%fused_computation.73 | loop fusion | flops 20971520 | bytes 33554432 | tf_op jit(solution)/shard_map/neg | solution.py:21
  114.0 0.2 sine_multiply_fusion
  114.1 0.2 negate_convert_fusion
  114.3 0.0 copy-done.4
  114.4 20.7 %maximum_bitcast_fusion = bf16[16,1,64,64,128]{4,2,1,3,0:T(8,128)(2,1)} fusion(bf16[16,64,64,64]{3,1,2,0:T(8,128)(2,1)} %bitcast.92, bf16[16,64,64,64]{3,1,2,0:T(8,128)(2,1)} %bitcast.90), kind=kLoop, calls=%fused_computation.19 | loop fusion | flops 33554432 | bytes 33554432 | tf_op jit(solution)/shard_map/stack | solution.py:25
  135.1 23.3 %bitcast_convert_fusion.1 = bf16[16,64,128,64]{2,3,1,0:T(8,128)(2,1)} fusion(bf16[16,1,64,64,128]{4,2,1,3,0:T(8,128)(2,1)} %maximum_bitcast_fusion, bf16[16,1,64,64,64]{4,2,1,3,0:T(8,128)(2,1)} %bitcast.91, bf16[16,1,64,64,64]{4,2,1,3,0:T(8,128)(2,1)} %bitcast.95, bf16[1,64,64]{2,1,0:T(8,128)(2,1)S(1)} %get-tuple-element.20, ...), kind=kOutput, calls=%fused_computation.10 | convolution fusion | flops 2256568320 | bytes 50348032 | tf_op jit(solution)/shard_map/ikx,bixym->bkym/dot_general | solution.py:26
  158.4 25.0 %fusion.47 = (bf16[16,64,64,64]{3,1,2,0:T(8,128)(2,1)}, bf16[16,64,64,64]{3,1,2,0:T(8,128)(2,1)}) fusion(bf16[16,64,64,128]{3,1,2,0:T(8,128)(2,1)} %bitcast.82), kind=kLoop, calls=%fused_computation.74 | loop fusion | flops 4194304 | bytes 33554432 | tf_op jit(solution)/shard_map/slice | solution.py:21
  183.5 0.1 copy.26
  183.6 0.1 reshape.276
  183.7 20.7 %maximum_bitcast_fusion.1 = bf16[16,1,64,64,128]{4,2,3,0,1:T(8,128)(2,1)} fusion(bf16[16,64,64,64]{3,1,2,0:T(8,128)(2,1)} %get-tuple-element.11, bf16[16,64,64,64]{3,1,2,0:T(8,128)(2,1)} %get-tuple-element.10), kind=kLoop, calls=%fused_computation.20 | loop fusion | flops 33554432 | bytes 33554432 | tf_op jit(solution)/shard_map/stack | solution.py:25
  204.4 23.0 %pad_maximum_fusion = bf16[16,2,64,64,128]{4,2,3,0,1:T(8,128)(2,1)} fusion(bf16[16,1,64,64,128]{4,2,3,0,1:T(8,128)(2,1)} %maximum_bitcast_fusion.1, bf16[16,1,64,64,128]{4,2,3,0,1:T(8,128)(2,1)} %bitcast.83), kind=kLoop, calls=%fused_computation.8 | loop fusion | flops 16777216 | bytes 67108864 | tf_op jit(solution)/shard_map/stack | solution.py:25
  227.4 39.5 %fusion.17 = bf16[16,64,64,128]{3,2,1,0:T(8,128)(2,1)} fusion(bf16[16,2,64,64,128]{4,2,3,0,1:T(8,128)(2,1)} %pad_maximum_fusion, bf16[128,128,1,1]{1,0,2,3:T(8,128)(2,1)S(1)} %reshape.276, bf16[1,64,64]{2,1,0:T(8,128)(2,1)S(1)} %get-tuple-element.20, bf16[1,64,64]{2,1,0:T(8,128)(2,1)S(1)} %get-tuple-element.21), kind=kOutput, calls=%fused_computation.25 | convolution fusion | flops 4311777280 | bytes 50380800 | tf_op jit(solution)/shard_map/bxym,mn->bxyn/dot_general | solution.py:60
  267.0 13.9 %reshape.249 = bf16[4,4,524288]{2,1,0:T(4,128)(2,1)} reshape(bf16[16,64,64,128]{3,2,1,0:T(8,128)(2,1)} %fusion.17) | data formatting | bytes 33554432 | tf_op jit(solution)/shard_map/reshape | solution.py:63
  280.9 148.6 %gather_fusion = bf16[10240,4,4]{0,2,1:T(4,128)(2,1)S(1)} fusion(bf16[4,4,524288]{2,1,0:T(4,128)(2,1)} %reshape.249, s32[10240]{0:T(1024)S(1)} %get-tuple-element.18), kind=kCustom, calls=%fused_computation.clone | custom fusion | bytes 696320 | tf_op jit(solution)/shard_map/jit(_take)/gather | solution.py:67
  429.4 0.0 copy-start.5
  429.5 0.0 copy-start.6
  429.5 0.0 copy-start.7
  429.5 0.0 copy-start.8
  429.5 149.0 %gather_fusion.1 = bf16[10240,4,4]{0,2,1:T(4,128)(2,1)S(1)} fusion(bf16[4,4,524288]{2,1,0:T(4,128)(2,1)} %reshape.249, s32[10240]{0:T(1024)S(1)} %get-tuple-element.19), kind=kCustom, calls=%fused_computation.1.clone | custom fusion | bytes 696320 | tf_op jit(solution)/shard_map/jit(_take)/gather | solution.py:67
  578.5 0.2 select_bitcast_fusion.1
  578.7 0.2 select_bitcast_fusion
  578.9 0.5 pad_maximum_fusion.2
  579.3 1.4 copy.29
  580.7 0.0 all-gather.5.cloned.1.call-update
  580.7 0.0 copy-done.5
  580.7 0.0 copy-done.6
  580.7 0.0 copy-done.7
  580.8 0.0 copy-done.8
  580.8 0.1 fusion.42
  580.8 0.4 multiply_convert_fusion
  581.2 19.5 %copy.27 = bf16[4,4,2,10240]{1,0,2,3:T(4,128)(2,1)} copy(bf16[4,4,2,10240]{3,1,0,2:T(4,128)(2,1)S(1)} %multiply_convert_fusion) | data formatting | bytes 1310720 | tf_op jit(solution)/shard_map/convert_element_type | solution.py:77
  600.7 40.7 %reshape.280 = bf16[16,2,10240]{2,1,0:T(2,128)(2,1)} reshape(bf16[10240,2,4,4]{3,2,1,0:T(4,128)(2,1)} %bitcast.84) | data formatting | bytes 1310720
  641.4 7.4 all-to-all-start
  648.8 34.4 %all-gather.5.cloned.1.call-done = bf16[4,64,2,10240]{3,0,2,1:T(4,128)(2,1)} async-done(((bf16[4,4,2,10240]{3,0,2,1:T(4,128)(2,1)}), bf16[4,64,2,10240]{3,0,2,1:T(4,128)(2,1)}) %all-gather.5.cloned.1.call-update) | async-done | bytes 10485776 | tf_op jit(solution)/shard_map/all_gather | solution.py:80
  683.2 33.4 %copy.30 = bf16[4,64,2,10240]{1,0,2,3:T(4,128)(2,1)} copy(bf16[4,64,2,10240]{3,0,2,1:T(4,128)(2,1)} %all-gather.5.cloned.1.call-done) | data formatting | bytes 20971520 | tf_op jit(solution)/shard_map/all_gather | solution.py:80
  716.6 29.0 %reshape.282 = bf16[2,2,1310720]{2,1,0:T(2,128)(2,1)} reshape(bf16[10240,2,4,64]{3,2,1,0:T(4,128)(2,1)} %bitcast.86) | data formatting | bytes 20971520
  745.6 0.0 all-to-all-done
  745.6 7.7 all-to-all-start.1
  753.3 0.0 all-gather.3.cloned.1.call-start
  753.3 46.4 %reshape.281 = bf16[10240,2,4,4]{3,2,1,0:T(4,128)(2,1)} reshape(bf16[16,2,10240]{2,1,0:T(2,128)(2,1)S(1)} %all-to-all-done) | data formatting | bytes 1310720
  799.7 25.9 %copy.28 = bf16[4,16,4,2,640]{4,2,1,3,0:T(4,128)(2,1)S(1)} copy(bf16[4,16,4,2,640]{2,0,3,4,1:T(4,128)(2,1)} %bitcast.85) | data formatting | bytes 1310720 | tf_op jit(solution)/shard_map/all_to_all | solution.py:78
  825.6 1.0 all_to_all.29
  826.6 0.0 all-gather.3.cloned.1.call-update
  826.7 56.1 %all-to-all-done.1 = bf16[2,2,1310720]{2,1,0:T(2,128)(2,1)} async-done(((bf16[2,2,1310720]{2,1,0:T(2,128)(2,1)}), bf16[2,2,1310720]{2,1,0:T(2,128)(2,1)}, u32[]{:S(2)}, u32[]{:S(2)}) %all-to-all-start.1) | async-done | bytes 10485792 | tf_op jit(solution)/shard_map/all_to_all | solution.py:81
  882.8 28.6 %reshape.283 = bf16[10240,2,4,64]{3,2,1,0:T(4,128)(2,1)} reshape(bf16[2,2,1310720]{2,1,0:T(2,128)(2,1)} %all-to-all-done.1) | data formatting | bytes 20971520
  911.5 30.1 %copy.31 = bf16[4,64,2,2,5120]{4,1,2,0,3:T(8,128)(2,1)} copy(bf16[4,64,2,2,5120]{1,0,2,4,3:T(4,128)(2,1)} %bitcast.87) | data formatting | bytes 20971520 | tf_op jit(solution)/shard_map/all_to_all | solution.py:81
  941.6 8.8 slice_negate_fusion.1
  950.4 10.3 %convolution_bitcast_fusion = f32[1,640,5120]{2,1,0:T(8,128)S(1)} fusion(bf16[8,64,2,640]{3,1,2,0:T(8,128)(2,1)} %all-gather.3.cloned.1.call-done, bf16[8,64,2,5120]{3,1,2,0:T(8,128)(2,1)} %bitcast.94), kind=kOutput, calls=%fused_computation.27 | convolution fusion | flops 6710886400 | bytes 24903680 | tf_op jit(solution)/shard_map/dot_general | solution.py:34
  960.7 10.2 %fusion.20 = f32[1,640,5120]{2,1,0:T(8,128)} fusion(bf16[8,64,2,640]{3,1,2,0:T(8,128)(2,1)S(1)} %copy-done.9, bf16[8,64,1,5120]{3,1,2,0:T(8,128)(2,1)S(1)} %copy-done.3, bf16[8,64,1,5120]{3,1,2,0:T(8,128)(2,1)S(1)} %copy-done.2), kind=kOutput, calls=%fused_computation.26 | convolution fusion | flops 6716129280 | bytes 24903680 | tf_op jit(solution)/shard_map/dot_general | solution.py:35
  970.9 14.5 %pad_maximum_fusion.1 = f32[2,640,5120]{2,1,0:T(8,128)} fusion(f32[1,640,5120]{2,1,0:T(8,128)} %fusion.20, f32[1,640,5120]{2,1,0:T(8,128)S(1)} %convolution_bitcast_fusion), kind=kLoop, calls=%fused_computation.15 | loop fusion | flops 6553600 | bytes 52428800 | tf_op jit(solution)/shard_map/stack | solution.py:36
  (17 shorter events, 0.1 us)
Async XLA Ops:
  7.4 675.8 %all-gather.5.cloned.1.call-start = ((), (), s32[]{:S(2)}) async-start(), calls=%async_computation.3 | async-start | bytes 11141120 | tf_op jit(solution)/shard_map/all_gather | solution.py:80
  7.4 22.8 %copy-start.1 = (bf16[4,64,64,128]{3,2,1,0:T(8,128)(2,1)S(1)}, bf16[4,64,64,128]{3,2,1,0:T(8,128)(2,1)}, u32[]{:S(2)}) copy-start(bf16[4,64,64,128]{3,2,1,0:T(8,128)(2,1)} %param.10) | copy-start | bytes 12582916
  46.4 26.6 %copy-start = (f32[4,64,64,64]{3,1,2,0:T(8,128)}, f32[4,64,64,64]{3,1,2,0:T(8,128)S(1)}, u32[]{:S(2)}) copy-start(f32[4,64,64,64]{3,1,2,0:T(8,128)S(1)} %copy.22) | copy-start | bytes 12582916
  46.4 26.5 %slice-start = ((s8[8388608]{0:T(1024)(128)(4,1)}), s8[4194304]{0:T(1024)(128)(4,1)S(1)}, s32[]{:S(2)}) async-start(s8[8388608]{0:T(1024)(128)(4,1)} %bitcast.88), calls=%async_computation.4 | async-start | bytes 8388608
  60.9 12.0 %slice-start.1 = ((s8[8388608]{0:T(1024)(128)(4,1)}), s8[4194304]{0:T(1024)(128)(4,1)S(1)}, s32[]{:S(2)}) async-start(s8[8388608]{0:T(1024)(128)(4,1)} %bitcast.88), calls=%async_computation.5 | async-start | bytes 8388608
  88.2 26.1 %copy-start.4 = (s32[10240]{0:T(1024)S(1)}, s32[10240]{0:T(1024)}, u32[]{:S(2)}) copy-start(s32[10240]{0:T(1024)} %param.15) | copy-start | bytes 122884
  429.4 151.3 %copy-start.5 = (f32[4]{0:T(128)S(1)}, f32[4]{0:T(128)}, u32[]{:S(2)}) copy-start(f32[4]{0:T(128)} %param.12) | copy-start | bytes 52
  429.5 151.3 %copy-start.6 = (f32[4]{0:T(128)S(1)}, f32[4]{0:T(128)}, u32[]{:S(2)}) copy-start(f32[4]{0:T(128)} %param.11) | copy-start | bytes 52
  429.5 151.3 %copy-start.7 = (s32[4]{0:T(128)S(1)}, s32[4]{0:T(128)}, u32[]{:S(2)}) copy-start(s32[4]{0:T(128)} %param.14) | copy-start | bytes 52
  429.5 151.3 %copy-start.8 = (s32[4]{0:T(128)S(1)}, s32[4]{0:T(128)}, u32[]{:S(2)}) copy-start(s32[4]{0:T(128)} %param.13) | copy-start | bytes 52
  641.4 104.2 %all-to-all-start = ((bf16[16,2,10240]{2,1,0:T(2,128)(2,1)}), bf16[16,2,10240]{2,1,0:T(2,128)(2,1)S(1)}, u32[]{:S(2)}, u32[]{:S(2)}) async-start(bf16[16,2,10240]{2,1,0:T(2,128)(2,1)} %reshape.280), calls=%async_computation | async-start | bytes 1310720 | tf_op jit(solution)/shard_map/all_to_all | solution.py:78
  745.6 137.2 %all-to-all-start.1 = ((bf16[2,2,1310720]{2,1,0:T(2,128)(2,1)}), bf16[2,2,1310720]{2,1,0:T(2,128)(2,1)}, u32[]{:S(2)}, u32[]{:S(2)}) async-start(bf16[2,2,1310720]{2,1,0:T(2,128)(2,1)} %reshape.282), calls=%async_computation.1 | async-start | bytes 20971520 | tf_op jit(solution)/shard_map/all_to_all | solution.py:81
  753.3 197.1 %all-gather.3.cloned.1.call-start = ((), (), s32[]{:S(2)}) async-start(), calls=%async_computation.2 | async-start | bytes 1966080 | tf_op jit(solution)/shard_map/all_gather | solution.py:79
  950.4 10.3 %copy-start.2 = (bf16[8,64,1,5120]{3,1,2,0:T(8,128)(2,1)S(1)}, bf16[8,64,1,5120]{3,1,2,0:T(8,128)(2,1)}, u32[]{:S(2)}) copy-start(bf16[8,64,1,5120]{3,1,2,0:T(8,128)(2,1)} %get-tuple-element.12) | copy-start | bytes 15728644
  950.4 10.3 %copy-start.3 = (bf16[8,64,1,5120]{3,1,2,0:T(8,128)(2,1)S(1)}, bf16[8,64,1,5120]{3,1,2,0:T(8,128)(2,1)}, u32[]{:S(2)}) copy-start(bf16[8,64,1,5120]{3,1,2,0:T(8,128)(2,1)} %get-tuple-element.13) | copy-start | bytes 15728644
  950.4 10.3 %copy-start.9 = (bf16[8,64,2,640]{3,1,2,0:T(8,128)(2,1)S(1)}, bf16[8,64,2,640]{3,1,2,0:T(8,128)(2,1)}, u32[]{:S(2)}) copy-start(bf16[8,64,2,640]{3,1,2,0:T(8,128)(2,1)} %all-gather.3.cloned.1.call-done) | copy-start | bytes 3932164
Sparse Core Ops, SparseCore 0:
  580.8 102.2 all-gather.4
Sparse Core Ops, SparseCore 1:
  826.8 37.6 all-gather.2
where the time goes:
time: 1010 us; the launch traced here: 993 us
  local copies, waits for them, and re-layouts  614 us (61%)
  other arithmetic  175 us (17%)
  waiting for transfers between devices  90.6 us (9%)
  matrix products  83.3 us (8%)
  between operations  15.3 us (2%)
  starting transfers between devices  15.1 us (1%)
    gather x1, local copies, waits for them, and re-layouts, local(): jnp.take(flat, base_pos + NG, axis=2)  149 us
    gather x1, local copies, waits for them, and re-layouts, local(): jnp.take(flat, base_pos, axis=2)  149 us
    unnamed x28, local copies, waits for them, and re-layouts  145 us
    another operation x3, other arithmetic, along_middle(): stacked = jnp.stack([field, swap_parts(field, grid)], axis=1)  64.5 us
    all_to_all x1, waiting for transfers between devices, local(): lax.all_to_all(all_cond, 'col', split_axis=3, concat_axis=0, tiled=True)  56.1 us
    dot_general x1, matrix products, local(): jnp.einsum('bxym,mn->bxyn', field, z_matrix, preferred_element_type=jnp.f...  39.5 us
    all_gather x1, waiting for transfers between devices, local(): all_cond = lax.all_gather(rho, 'band', axis=1, tiled=True)  34.4 us
    all_gather x1, local copies, waits for them, and re-layouts, local(): all_cond = lax.all_gather(rho, 'band', axis=1, tiled=True)  33.4 us
  transfers between devices with their start and end apart: 4, of which 2 were waited for; matrix products, arithmetic and copies ran while one was open for 26% of the time, Pallas kernels for 0%

commit v1 on v0

v1 whole, which is shorter than its diff:
```python
import functools
import math

import jax
import jax.numpy as jnp
import ml_dtypes
import numpy as np
from jax import lax
from jax.experimental import pallas as pl
from jax.experimental.pallas import tpu as pltpu
from jax.sharding import PartitionSpec as P

PAD = 32
VMEM = 56 * 1024 * 1024


def sphere(grid, count):
    comp = (np.arange(grid) + grid // 2) % grid - grid // 2
    square = comp * comp
    lengths = square[:, None, None] + square[None, :, None] + square[None, None, :]
    top = int(np.sort(lengths.ravel())[count - 1])
    reach = math.isqrt(top)
    widths = [2 * math.isqrt(top - k * k) + 1 for k in range(-reach, reach + 1)]
    offsets = [0]
    for width in widths:
        offsets.append(offsets[-1] + width)
    return reach, offsets


def tables(grid, reach):
    freq = np.arange(PAD) - reach
    kept = (np.arange(PAD) < 2 * reach + 1).astype(np.float64)
    rank = np.arange(PAD)
    ranked = (rank + 1) // 2 * np.where(rank % 2 == 1, 1, -1)

    def pair(values):
        angle = 2.0 * math.pi / grid * ((values[:, None] * np.arange(grid)[None, :]) % grid)
        return (
            np.cos(angle) / math.sqrt(grid) * kept[:, None],
            np.sin(angle) / math.sqrt(grid) * kept[:, None],
        )

    cosine, sine = pair(freq)
    full = np.array([[cosine, sine], [-sine, cosine]])
    swapped = np.array([full[1], -full[0]])
    z_block = np.zeros((2, 2, grid, 2, PAD, 2, 2))
    for member in range(2):
        for which, part in enumerate((full, swapped)):
            z_block[member, :, :, which, :, member, :] = np.transpose(part, (1, 3, 2, 0))
    z_matrix = z_block.reshape(4 * grid, 8 * PAD)
    one = np.array([[cosine, sine], [-sine, cosine]])
    y_block = np.zeros((2, 2, PAD, 2, 2, grid))
    for member in range(2):
        y_block[member, :, :, member] = np.transpose(one, (0, 2, 1, 3))
    y_matrix = y_block.reshape(4 * PAD, 4 * grid)
    cos_x, sin_x = pair(ranked)
    x_block = np.zeros((2, PAD, 2, grid, 2))
    for member in range(2):
        x_block[member, :, member] = np.stack([cos_x, sin_x], axis=-1)
    x_matrix = x_block.reshape(2 * PAD, 4 * grid)
    return [m.astype(ml_dtypes.bfloat16) for m in (z_matrix, y_matrix, x_matrix)]


def transform_kernel(
    grid, offsets, packed, val_ref, cond_ref, z_ref, y_ref, x_ref, out_ref, mid, cols
):
    half = 2 * PAD * 2
    lane = lax.broadcasted_iota(jnp.int32, (2 * grid, 2 * grid), 1)
    low = lane < grid

    def planes(step, carry):
        val = val_ref[0, pl.ds(step * 2, 2)].reshape(2 * grid, 2 * grid).astype(jnp.float32)
        turned = pltpu.roll(val, grid, 1)
        val_re = jnp.where(low, val, turned)
        val_im = jnp.where(low, turned, -val)
        fields = []
        for band in range(4):
            cond = cond_ref[band, pl.ds(step * 2, 2)].reshape(2 * grid, 2 * grid)
            cond = cond.astype(jnp.float32)
            product = val_re * cond + val_im * pltpu.roll(cond, grid, 1)
            fields.append(product.astype(jnp.bfloat16))
        parts = []
        for first in (0, 2):
            both = jnp.concatenate(fields[first : first + 2], axis=1)
            parts.append(
                jnp.dot(both, z_ref[...], preferred_element_type=jnp.float32).astype(jnp.bfloat16)
            )
        stacked = []
        for plane in range(2):
            rows = slice(plane * grid, (plane + 1) * grid)
            for which in range(2):
                lanes = slice(which * half, (which + 1) * half)
                stacked.append(
                    jnp.concatenate([parts[0][rows, lanes], parts[1][rows, lanes]], axis=1)
                )
        stacked = jnp.concatenate(stacked, axis=0)
        found = jnp.dot(y_ref[...], stacked, preferred_element_type=jnp.float32)
        start = pl.multiple_of(step * 4 * PAD, 4 * PAD)
        for side in range(2):
            mid[side, pl.ds(start, 4 * PAD), :] = found[:, side * half : (side + 1) * half]
        return carry

    lax.fori_loop(0, grid // 2, planes, 0)
    cols[...] = jnp.zeros_like(cols)
    count = len(offsets) - 1
    for first in range(0, count, 2):
        rows = [
            jnp.concatenate(
                [
                    mid[side, pl.ds(first + member, 2 * grid, stride=PAD), :].astype(jnp.bfloat16)
                    for side in range(2)
                ],
                axis=1,
            )
            for member in range(2)
        ]
        found = jnp.dot(
            x_ref[...], jnp.concatenate(rows, axis=0), preferred_element_type=jnp.float32
        )
        for member in range(2):
            if first + member < count:
                start = offsets[first + member]
                cols[start : start + PAD, :] = found[member * PAD : (member + 1) * PAD]
    turned = cols[...].T
    for k in range(PAD):
        out_ref[k, 0:4, :] = turned[4 * k : 4 * k + 4]
        out_ref[k, 4:8, :] = turned[half + 4 * k : half + 4 * k + 4]


def pick_kernel(count, rows, packed, field_ref, col_ref, sel_ref, out_ref, held):
    @pl.when(pl.program_id(0) == 0)
    def _():
        held[...] = field_ref[0:count].reshape(count * rows, packed).astype(jnp.bfloat16)

    tile = out_ref.shape[1]
    place = lax.broadcasted_iota(jnp.int32, (packed, tile), 0)
    chosen = jnp.where(place == col_ref[...], 1.0, 0.0).astype(jnp.bfloat16)
    found = jnp.dot(held[...], chosen, preferred_element_type=jnp.float32)
    select = jnp.broadcast_to(sel_ref[...], (rows, tile))
    total = jnp.zeros((rows, tile), jnp.float32)
    for k in range(count):
        total = total + jnp.where(select == k, found[k * rows : (k + 1) * rows], 0.0)
    out_ref[...] = total.astype(jnp.bfloat16)


def densities(valence, conduction, gvec_index):
    val_local, grid = valence.shape[0], valence.shape[1]
    npw = gvec_index.shape[0]
    reach, offsets = sphere(grid, npw)
    count = 2 * reach + 1
    assert count <= PAD and conduction.shape[0] == 4
    packed = -(-(offsets[-2] + PAD) // 128) * 128
    z_matrix, y_matrix, x_matrix = tables(grid, reach)
    features = 8 * val_local
    whole = lambda shape: pl.BlockSpec(shape, lambda v: (0,) * len(shape))
    field = pl.pallas_call(
        functools.partial(transform_kernel, grid, offsets, packed),
        grid=(val_local,),
        in_specs=[
            pl.BlockSpec((1, grid, grid, 2 * grid), lambda v: (v, 0, 0, 0)),
            whole(conduction.shape),
            whole(z_matrix.shape),
            whole(y_matrix.shape),
            whole(x_matrix.shape),
        ],
        out_specs=pl.BlockSpec((PAD, 8, packed), lambda v: (0, v, 0)),
        out_shape=jax.ShapeDtypeStruct((PAD, features, packed), jnp.float32),
        scratch_shapes=[
            pltpu.VMEM((2, 2 * grid * PAD, 4 * PAD), jnp.float32),
            pltpu.VMEM((packed, 8 * PAD), jnp.float32),
        ],
        compiler_params=pltpu.CompilerParams(vmem_limit_bytes=VMEM),
        name="transform",
    )(valence, conduction, z_matrix, y_matrix, x_matrix)

    half = grid // 2
    wrap = lambda part: (part + half) % grid - half
    x_comp = wrap(gvec_index // (grid * grid))
    y_comp = wrap(gvec_index // grid % grid)
    z_comp = wrap(gvec_index % grid)
    col = jnp.where(x_comp > 0, 2 * x_comp - 1, -2 * x_comp)
    for k in range(count):
        col = col + jnp.where(y_comp == k - reach, offsets[k], 0)
    tile = 256
    return pl.pallas_call(
        functools.partial(pick_kernel, count, features, packed),
        grid=(npw // tile,),
        in_specs=[
            whole((PAD, features, packed)),
            pl.BlockSpec((1, tile), lambda g: (0, g)),
            pl.BlockSpec((1, tile), lambda g: (0, g)),
        ],
        out_specs=pl.BlockSpec((features, tile), lambda g: (0, g)),
        out_shape=jax.ShapeDtypeStruct((features, npw), jnp.bfloat16),
        scratch_shapes=[pltpu.VMEM((count * features, packed), jnp.bfloat16)],
        compiler_params=pltpu.CompilerParams(vmem_limit_bytes=VMEM),
        name="pick",
    )(field, col[None], (z_comp + reach)[None])


def pair_weights(energy_valence, energy_conduction, occ_valence, occ_conduction):
    total_val = energy_valence.shape[0] * lax.axis_size("col")
    total_cond = energy_conduction.shape[0] * lax.axis_size("band")
    occ_diff = (occ_valence[:, None] - occ_conduction[None, :]).astype(jnp.float32)
    return (
        occ_diff
        / (energy_valence[:, None] - energy_conduction[None, :])
        / math.sqrt(total_val * total_cond)
    )


def local(
    valence, conduction, energy_valence, energy_conduction, occ_valence, occ_conduction, gvec_index
):
    rho = densities(valence, conduction, gvec_index)
    features, npw = rho.shape
    weight = pair_weights(energy_valence, energy_conduction, occ_valence, occ_conduction)
    weight = jnp.repeat(weight.reshape(-1), 2)
    weighted = (weight[:, None] * rho.astype(jnp.float32)).astype(jnp.bfloat16)
    cols = lax.all_to_all(rho, "col", split_axis=1, concat_axis=0, tiled=True)
    cols = lax.all_gather(cols, "band", axis=0, tiled=True)
    rows = lax.all_to_all(weighted, "band", split_axis=1, concat_axis=0, tiled=True)
    rows = lax.all_gather(rows, "col", axis=0, tiled=False)
    n_col, n_band = lax.axis_size("col"), lax.axis_size("band")
    rows = rows.reshape(n_col, n_band, features // 2, 2, npw // n_band)
    rows = jnp.transpose(rows, (1, 0, 2, 3, 4))
    turned = jnp.stack([rows[:, :, :, 1], -rows[:, :, :, 0]], axis=3)
    depth = n_col * n_band * features
    both = jnp.concatenate(
        [rows.reshape(depth, npw // n_band), turned.reshape(depth, npw // n_band)], axis=1
    )
    tile = lax.dot_general(
        both, cols, (((0,), (0,)), ((), ())), preferred_element_type=jnp.float32
    )
    return tile.reshape(2, npw // n_band, cols.shape[1])


def solution(mesh):
    return jax.shard_map(
        local,
        mesh=mesh,
        in_specs=(
            P("col", None, None, None),
            P("band", None, None, None),
            P("col"),
            P("band"),
            P("col"),
            P("band"),
            P(),
        ),
        out_specs=P(None, "band", "col"),
        check_vma=False,
    )
```

time: 1010 us -> 271 us (0.27)
  the two profiles are of different devices: /device:TPU:0 before, /device:TPU:8 now
where the time goes in v1:
time: 271 us; the launch traced here: 268 us
  Pallas kernels  89.9 us (33%)
  waiting for transfers between devices  85.6 us (32%)
  blocking collectives  41.2 us (15%)
  matrix products  21.9 us (8%)
  between operations  13.5 us (5%)
  other arithmetic  9.02 us (3%)
  local copies, waits for them, and re-layouts  6.53 us (2%)
    all_gather x1, waiting for transfers between devices, local(): cols = lax.all_gather(cols, 'band', axis=0, tiled=True)  75.9 us
    pallas_call x1, Pallas kernels, densities(): pl.pallas_call(functools.partial(transform_kernel, grid, offsets, packed)...  63.1 us
    pallas_call x1, Pallas kernels, densities(): pl.pallas_call(functools.partial(pick_kernel, count, features, packed), g...  26.7 us
    all_to_all x1, blocking collectives, local(): lax.all_to_all(weighted, 'band', split_axis=1, concat_axis=0, tiled=True)  23.5 us
    dot_general x1, matrix products, local(): lax.dot_general(both, cols, (((0,), (0,)), ((), ())), preferred_element_t...  21.9 us
    all_to_all x1, blocking collectives, local(): cols = lax.all_to_all(rho, 'col', split_axis=1, concat_axis=0, tiled=True)  17.6 us
    all_gather x1, waiting for transfers between devices, local(): rows = lax.all_gather(rows, 'col', axis=0, tiled=False)  9.68 us
  transfers between devices with their start and end apart: 2, of which 2 were waited for; matrix products, arithmetic and copies ran while one was open for 4% of the time, Pallas kernels for 0%

profile of v1, /device:TPU:8, one launch (start us, length us, event | category | flops | bytes accessed | tf_op | source)
XLA Modules:
  0.0 267.6 jit_solution(6582383711498436751)
XLA Ops:
  6.5 0.0 all-gather.3.cloned.1.call-start
  6.5 0.8 fusion.17
  7.3 0.1 div.34
  7.4 0.1 broadcast_in_dim.121
  7.5 0.1 mul.16
  7.6 1.6 fusion.14
  9.2 63.1 %transform.1.field_ref = f32[32,32,640]{2,1,0:T(8,128)} custom-call(bf16[4,64,64,128]{3,2,1,0:T(8,128)(2,1)} %val_ref.1, bf16[4,64,64,128]{3,2,1,0:T(8,128)(2,1)} %cond_ref.1, bf16[256,256]{1,0:T(8,128)(2,1)} %constant.177.clone.z_ref, bf16[128,256]{1,0:T(8,128)(2,1)} %constant.178.clone.y_ref, bf16[64,256]{1,0:T(8,128)(2,1)} %constant.179.clone.x_ref), custom_call_target="tpu_custom_call" | custom-call | tf_op jit(solution)/shard_map/transform/pallas_call | solution.py:156
  72.4 26.7 %pick.1 = bf16[32,10240]{1,0:T(8,128)(2,1)} custom-call(f32[32,32,640]{2,1,0:T(8,128)} %transform.1.field_ref, s32[1,10240]{1,0:T(1,128)} %bitcast.30, s32[1,10240]{1,0:T(1,128)} %bitcast.29), custom_call_target="tpu_custom_call" | custom-call | tf_op jit(solution)/shard_map/pick/pallas_call | solution.py:185
  99.1 1.3 multiply_convert_fusion
  100.3 0.1 copy.24
  100.4 0.0 copy-start
  100.4 23.5 %all_to_all.35 = bf16[32,16,640]{2,0,1:T(8,128)(2,1)} all-to-all(bf16[32,16,640]{2,0,1:T(8,128)(2,1)S(1)} %bitcast.27), channel_id=1, replica_groups=mesh['band'=16,'col'=2] {'band'}, dimensions={1} | all-to-all | bytes 1310720 | tf_op jit(solution)/shard_map/all_to_all | solution.py:222
  123.9 0.0 all-gather.3.cloned.1.call-update
  124.0 0.0 all-gather.5.cloned.1.call-start
  124.0 0.0 copy-done
  124.1 17.6 %all_to_all.36 = bf16[32,2,5120]{2,0,1:T(8,128)(2,1)} all-to-all(bf16[32,2,5120]{2,0,1:T(8,128)(2,1)S(1)} %bitcast.28), channel_id=1, replica_groups=mesh['band'=16,'col'=2] {'col'}, dimensions={1} | all-to-all | bytes 1310720 | tf_op jit(solution)/shard_map/all_to_all | solution.py:220
  141.7 0.0 all-gather.5.cloned.1.call-update
  141.7 9.7 %all-gather.3.cloned.1.call-done = bf16[2,512,640]{2,1,0:T(8,128)(2,1)} async-done(((bf16[1,512,640]{2,1,0:T(8,128)(2,1)}), bf16[2,512,640]{2,1,0:T(8,128)(2,1)}) %all-gather.3.cloned.1.call-update) | async-done | bytes 1310736 | tf_op jit(solution)/shard_map/all_gather | solution.py:223
  151.4 3.1 %reshape.35 = bf16[2,16,16,2,640]{4,3,2,1,0:T(2,128)(2,1)S(1)} reshape(bf16[2,512,640]{2,1,0:T(8,128)(2,1)} %all-gather.3.cloned.1.call-done) | data formatting | bytes 2621440 | tf_op jit(solution)/shard_map/reshape | solution.py:225
  154.5 1.2 copy.22
  155.7 0.5 reshape.36
  156.2 2.4 fusion.19
  158.6 3.0 %pad_maximum_fusion = bf16[16,2,16,2,640]{4,3,2,1,0:T(2,128)(2,1)S(1)} fusion(bf16[16,2,16,1,640]{4,3,2,1,0:T(2,128)(2,1)S(1)} %get-tuple-element.6, bf16[16,2,16,1,640]{4,3,2,1,0:T(2,128)(2,1)S(1)} %get-tuple-element.5), kind=kLoop, calls=%fused_computation.5 | loop fusion | flops 2621440 | bytes 2621440 | tf_op jit(solution)/shard_map/stack | solution.py:227
  161.6 1.4 reshape.37
  163.0 75.9 %all-gather.5.cloned.1.call-done = bf16[1024,5120]{1,0:T(8,128)(2,1)} async-done(((bf16[64,5120]{1,0:T(8,128)(2,1)}), bf16[1024,5120]{1,0:T(8,128)(2,1)}) %all-gather.5.cloned.1.call-update) | async-done | bytes 10485776 | tf_op jit(solution)/shard_map/all_gather | solution.py:221
  238.9 21.9 %fusion = f32[1280,5120]{1,0:T(8,128)} fusion(bf16[1024,5120]{1,0:T(8,128)(2,1)} %all-gather.5.cloned.1.call-done, bf16[1024,640]{1,0:T(8,128)(2,1)} %reshape.37, bf16[1024,640]{1,0:T(8,128)(2,1)S(1)} %reshape.36), kind=kOutput, calls=%fused_computation | convolution fusion | flops 13427015680 | bytes 39321600 | tf_op jit(solution)/shard_map/dot_general | solution.py:232
  (1 shorter events, 0.0 us)
Async XLA Ops:
  6.5 144.9 %all-gather.3.cloned.1.call-start = ((), (), s32[]{:S(2)}) async-start(), calls=%async_computation.2 | async-start | bytes 1966080 | tf_op jit(solution)/shard_map/all_gather | solution.py:223
  100.4 23.6 %copy-start = (bf16[32,10240]{1,0:T(8,128)(2,1)S(1)}, bf16[32,10240]{1,0:T(8,128)(2,1)}, u32[]{:S(2)}) copy-start(bf16[32,10240]{1,0:T(8,128)(2,1)} %pick.1) | copy-start | bytes 1966084
  124.0 114.9 %all-gather.5.cloned.1.call-start = ((), (), s32[]{:S(2)}) async-start(), calls=%async_computation.3 | async-start | bytes 11141120 | tf_op jit(solution)/shard_map/all_gather | solution.py:221
Sparse Core Ops, SparseCore 0:
  124.1 27.2 all-gather.2
  153.7 85.1 all-gather.4

commit v2 on v1

--- a/solution.py
+++ b/solution.py
@@ -127,20 +127,206 @@
         out_ref[k, 4:8, :] = turned[half + 4 * k : half + 4 * k + 4]
 
 
-def pick_kernel(count, rows, packed, field_ref, col_ref, sel_ref, out_ref, held):
-    @pl.when(pl.program_id(0) == 0)
-    def _():
-        held[...] = field_ref[0:count].reshape(count * rows, packed).astype(jnp.bfloat16)
-
-    tile = out_ref.shape[1]
+def pick_tile(count, rows, packed, held, col, sel):
+    tile = col.shape[1]
     place = lax.broadcasted_iota(jnp.int32, (packed, tile), 0)
-    chosen = jnp.where(place == col_ref[...], 1.0, 0.0).astype(jnp.bfloat16)
+    chosen = jnp.where(place == col, 1.0, 0.0).astype(jnp.bfloat16)
     found = jnp.dot(held[...], chosen, preferred_element_type=jnp.float32)
-    select = jnp.broadcast_to(sel_ref[...], (rows, tile))
+    select = jnp.broadcast_to(sel, (rows, tile))
     total = jnp.zeros((rows, tile), jnp.float32)
     for k in range(count):
         total = total + jnp.where(select == k, found[k * rows : (k + 1) * rows], 0.0)
-    out_ref[...] = total.astype(jnp.bfloat16)
+    return total.astype(jnp.bfloat16)
+
+
+def gather_kernel(
+    plan, field_ref, col_ref, sel_ref, all_ref, row_ref, held, stage,
+    x_send, x_recv, x_local, send, recv, r_send, r_recv, r_local,
+):
+    count, rows, packed, n_band, n_col, chunks, width, tile, share, window = plan
+    n_z = n_band // 4
+    me = lax.axis_index("band")
+    my_col = lax.axis_index("col")
+    z, y, core = me // 4, me // 2 % 2, me % 2
+    y_peer = z * 4 + (1 - y) * 2 + core
+    core_peer = z * 4 + y * 2 + 1 - core
+    span = chunks * width
+
+    def remote(src, dst, send_sem, recv_sem, **target):
+        return pltpu.make_async_remote_copy(
+            src_ref=src,
+            dst_ref=dst,
+            send_sem=send_sem,
+            recv_sem=recv_sem,
+            device_id=target,
+            device_id_type=pl.DeviceIdType.MESH,
+        )
+
+    def inside(value):
+        return (value >= 0) & (value < n_z)
+
+    barrier = pltpu.get_barrier_semaphore()
+
+    def greet(**target):
+        pl.semaphore_signal(
+            barrier, inc=1, device_id=target, device_id_type=pl.DeviceIdType.MESH
+        )
+
+    for step in (1, -1):
+        pl.when(inside(z + step))(functools.partial(greet, band=me + 4 * step))
+    greet(band=y_peer)
+    greet(band=core_peer)
+    for p in range(1, n_col):
+        greet(col=(my_col + p) % n_col)
+    known = (z > 0).astype(jnp.int32) + (z < n_z - 1).astype(jnp.int32) + 1 + n_col
+    pl.semaphore_wait(barrier, known)
+
+    held[...] = field_ref[0:count].reshape(count * rows, packed).astype(jnp.bfloat16)
+
+    def lanes(j):
+        return pl.ds(pl.multiple_of(j * width, 128), width)
+
+    def block(slot, j):
+        return all_ref.at[slot, :, :, lanes(j)]
+
+    def relay(slot, j, kind, target):
+        view = block(slot, j)
+        return remote(view, view, send.at[j, kind, slot], recv.at[j, slot], band=target)
+
+    def staged(j, owner):
+        return stage.at[:, pl.ds(pl.multiple_of(owner * span + j * width, 128), width)]
+
+    def across(j, p):
+        peer = (my_col + p) % n_col
+        return remote(
+            staged(j, peer),
+            all_ref.at[me, my_col, :, lanes(j)],
+            x_send.at[j, p],
+            x_recv.at[j, p],
+            col=peer,
+        )
+
+    def own(j):
+        return pltpu.make_async_copy(
+            staged(j, my_col), all_ref.at[me, my_col, :, lanes(j)], x_local.at[j]
+        )
+
+    def pick(j):
+        per = width // tile
+
+        def body(i, carry):
+            start = pl.multiple_of((i // per) * span + j * width + (i % per) * tile, 128)
+            where = pl.ds(start, tile)
+            stage[:, where] = pick_tile(
+                count, rows, packed, held, col_ref[:, where], sel_ref[:, where]
+            )
+            return carry
+
+        lax.fori_loop(0, n_col * per, body, 0)
+        own(j).start()
+        for p in range(1, n_col):
+            across(j, p).start()
+
+    def along_z(j, h, act):
+        if h == 0 and act == "start":
+            own(j).wait()
+            for p in range(1, n_col):
+                across(j, p).wait_recv()
+        for step in (1, -1):
+            source = z - step * h
+            slot = source * 4 + y * 2 + core
+
+            @pl.when(inside(source))
+            def _():
+                if h > 0 and act == "start":
+                    relay(slot, j, 2, y_peer).wait_recv()
+
+                @pl.when(inside(z + step))
+                def _():
+                    getattr(relay(slot, j, 0 if step == 1 else 1, me + 4 * step), act)()
+
+                if h > 0 or step == 1:
+                    getattr(relay(slot, j, 2, y_peer), act)()
+                    getattr(relay(slot, j, 3, core_peer), act)()
+
+    def along_y(j, h, act):
+        for step in (1, -1) if h > 0 else (1,):
+            source = z - step * h
+            slot = source * 4 + (1 - y) * 2 + core
+
+            @pl.when(inside(source))
+            def _():
+                copy = relay(slot, j, 3, core_peer)
+                if act == "start":
+                    copy.wait_recv()
+                getattr(copy, act)()
+
+    per_col = n_band // n_col
+    owner = me // per_col
+    base = me % per_col * share // 128 * 128
+
+    def row_copy(i, p):
+        return remote(
+            all_ref.at[:, :, :, pl.ds(pl.multiple_of(base + 128 * i, 128), 128)],
+            row_ref.at[:, :, :, pl.ds(128 * i, 128)],
+            r_send.at[i, p],
+            r_recv.at[i],
+            col=(my_col + p) % n_col,
+        )
+
+    def row_local(i):
+        return pltpu.make_async_copy(
+            all_ref.at[:, :, :, pl.ds(pl.multiple_of(base + 128 * i, 128), 128)],
+            row_ref.at[:, :, :, pl.ds(128 * i, 128)],
+            r_local.at[i],
+        )
+
+    def finish(j):
+        for other in range(2 * n_z):
+            slot = other * 2 + 1 - core
+            relay(slot, j, 3, core_peer).wait_recv()
+        for i in range(window // 128):
+
+            @pl.when((owner == my_col) & ((base + 128 * i) // width == j))
+            def _():
+                row_local(i).start()
+                for p in range(1, n_col):
+                    row_copy(i, p).start()
+
+    def tick(t, carry):
+        def at(lag, act):
+            j = t - lag
+            pl.when((j >= 0) & (j < chunks))(lambda: act(j))
+
+        at(0, pick)
+        at(n_z + 2, finish)
+        for h in range(n_z - 1, -1, -1):
+            at(2 + h, lambda j: along_y(j, h, "start"))
+            at(1 + h, lambda j: along_z(j, h, "start"))
+        return carry
+
+    lax.fori_loop(0, chunks + n_z + 2, tick, 0)
+
+    def settle(j, carry):
+        for p in range(1, n_col):
+            across(j, p).wait_send()
+        for h in range(n_z):
+            along_z(j, h, "wait_send")
+            along_y(j, h, "wait_send")
+        return carry
+
+    lax.fori_loop(0, chunks, settle, 0)
+    for i in range(window // 128):
+
+        @pl.when(owner == my_col)
+        def _():
+            row_local(i).wait()
+            for p in range(1, n_col):
+                row_copy(i, p).wait_send()
+
+        @pl.when(owner != my_col)
+        def _():
+            row_copy(i, 1).wait_recv()
 
 
 def densities(valence, conduction, gvec_index):
@@ -181,21 +367,51 @@
     col = jnp.where(x_comp > 0, 2 * x_comp - 1, -2 * x_comp)
     for k in range(count):
         col = col + jnp.where(y_comp == k - reach, offsets[k], 0)
-    tile = 256
-    return pl.pallas_call(
-        functools.partial(pick_kernel, count, features, packed),
-        grid=(npw // tile,),
-        in_specs=[
-            whole((PAD, features, packed)),
-            pl.BlockSpec((1, tile), lambda g: (0, g)),
-            pl.BlockSpec((1, tile), lambda g: (0, g)),
+    return field, col[None], (z_comp + reach)[None], count, packed
+
+
+def gathered(field, col, sel, count, packed):
+    features, npw = field.shape[1], col.shape[1]
+    n_band, n_col = lax.axis_size("band"), lax.axis_size("col")
+    chunks = 5
+    width = npw // n_col // chunks
+    tile = min(512, width)
+    share = npw // n_band
+    window = -(-share // 128) * 128
+    assert window >= share + max(share * r % 128 for r in range(n_band // n_col))
+    plan = (count, features, packed, n_band, n_col, chunks, width, tile, share, window)
+    vmem = pl.BlockSpec(memory_space=pltpu.VMEM)
+    dma = pltpu.SemaphoreType.DMA
+    pieces = window // 128
+    cols, rows = pl.pallas_call(
+        functools.partial(gather_kernel, plan),
+        in_specs=[vmem] * 3,
+        out_specs=[pl.BlockSpec(memory_space=pl.ANY)] * 2,
+        out_shape=[
+            jax.ShapeDtypeStruct((n_band, n_col, features, chunks * width), jnp.bfloat16),
+            jax.ShapeDtypeStruct((n_band, n_col, features, window), jnp.bfloat16),
         ],
-        out_specs=pl.BlockSpec((features, tile), lambda g: (0, g)),
-        out_shape=jax.ShapeDtypeStruct((features, npw), jnp.bfloat16),
-        scratch_shapes=[pltpu.VMEM((count * features, packed), jnp.bfloat16)],
-        compiler_params=pltpu.CompilerParams(vmem_limit_bytes=VMEM),
-        name="pick",
-    )(field, col[None], (z_comp + reach)[None])
+        scratch_shapes=[
+            pltpu.VMEM((count * features, packed), jnp.bfloat16),
+            pltpu.VMEM((features, npw), jnp.bfloat16),
+            dma((chunks, n_col)),
+            dma((chunks, n_col)),
+            dma((chunks,)),
+            dma((chunks, 4, n_band)),
+            dma((chunks, n_band)),
+            dma((pieces, n_col)),
+            dma((pieces,)),
+            dma((pieces,)),
+        ],
+        compiler_params=pltpu.CompilerParams(
+            vmem_limit_bytes=VMEM, collective_id=0, has_side_effects=True
+        ),
+        name="pick_and_gather",
+    )(field, col, sel)
+    if share % 128:
+        start = lax.axis_index("band") % (n_band // n_col) * share % 128
+        rows = lax.dynamic_slice_in_dim(rows, start, share, axis=3)
+    return cols, rows
 
 
 def pair_weights(energy_valence, energy_conduction, occ_valence, occ_conduction):
@@ -212,27 +428,22 @@
 def local(
     valence, conduction, energy_valence, energy_conduction, occ_valence, occ_conduction, gvec_index
 ):
-    rho = densities(valence, conduction, gvec_index)
-    features, npw = rho.shape
     weight = pair_weights(energy_valence, energy_conduction, occ_valence, occ_conduction)
-    weight = jnp.repeat(weight.reshape(-1), 2)
-    weighted = (weight[:, None] * rho.astype(jnp.float32)).astype(jnp.bfloat16)
-    cols = lax.all_to_all(rho, "col", split_axis=1, concat_axis=0, tiled=True)
-    cols = lax.all_gather(cols, "band", axis=0, tiled=True)
-    rows = lax.all_to_all(weighted, "band", split_axis=1, concat_axis=0, tiled=True)
-    rows = lax.all_gather(rows, "col", axis=0, tiled=False)
-    n_col, n_band = lax.axis_size("col"), lax.axis_size("band")
-    rows = rows.reshape(n_col, n_band, features // 2, 2, npw // n_band)
-    rows = jnp.transpose(rows, (1, 0, 2, 3, 4))
-    turned = jnp.stack([rows[:, :, :, 1], -rows[:, :, :, 0]], axis=3)
-    depth = n_col * n_band * features
-    both = jnp.concatenate(
-        [rows.reshape(depth, npw // n_band), turned.reshape(depth, npw // n_band)], axis=1
+    weight = lax.all_gather(weight.reshape(-1), ("band", "col"), axis=0, tiled=False)
+    cols, rows = gathered(*densities(valence, conduction, gvec_index))
+    n_band, n_col, features, share = rows.shape
+    depth = n_band * n_col * features
+    rows = rows.reshape(depth // 2, 2, share).astype(jnp.float32)
+    rows = (weight.reshape(-1)[:, None, None] * rows).astype(jnp.bfloat16)
+    turned = jnp.stack([rows[:, 1], -rows[:, 0]], axis=1)
+    both = jnp.concatenate([rows.reshape(depth, share), turned.reshape(depth, share)], axis=1)
+    tile = lax.dot_general(
+        both,
+        cols.reshape(depth, -1),
+        (((0,), (0,)), ((), ())),
+        preferred_element_type=jnp.float32,
     )
-    tile = lax.dot_general(
-        both, cols, (((0,), (0,)), ((), ())), preferred_element_type=jnp.float32
-    )
-    return tile.reshape(2, npw // n_band, cols.shape[1])
+    return tile.reshape(2, share, cols.shape[3])
 
 
 def solution(mesh):

time: 271 us -> 290 us (1.070)
  Pallas kernels: 89.9 us -> 186 us
  waiting for transfers between devices: 85.6 us -> 0 us
  between operations: 13.5 us -> 0.07 us
  blocking collectives: 41.2 us -> 54.2 us
  other arithmetic: 9.02 us -> 14.1 us
    pallas_call x1, Pallas kernels: 26.7 us -> 123 us  [gathered(): pl.pallas_call(functools.partial(gather_kernel, plan), in_specs=[vmem] *...]
    all_gather x2 -> x0, waiting for transfers between devices: 85.6 us -> none  [the longest x1 75.9 us: local(): cols = lax.all_gather(cols, 'band', axis=0, tiled=True)]
    all_gather x0 -> x1, blocking collectives: none -> 54.2 us  [local(): lax.all_gather(weight.reshape(-1), ('band', 'col'), axis=0, tiled=False)]
    all_to_all x2 -> x0, blocking collectives: 41.2 us -> none  [the longest x1 23.5 us: local(): lax.all_to_all(weighted, 'band', split_axis=1, concat_axis=0, tiled=True)]
    reshape x4 -> x1, local copies, waits for them, and re-layouts: 6.17 us -> 1.36 us  [local(): turned.reshape(depth, share)]
    convert_element_type x0 -> x1, local copies, waits for them, and re-layouts: none -> 3.07 us  [local(): rows = rows.reshape(depth // 2, 2, share).astype(jnp.float32)]
  transfers between devices with their start and end apart: 2 -> 0, of which waited for: 2 -> 0; matrix products, arithmetic and copies ran while one was open for 4% -> 0% of each run, Pallas kernels for 0% -> 0%
where the time goes in v2:
time: 290 us; the launch traced here: 285 us
  Pallas kernels  186 us (64%)
  blocking collectives  54.2 us (19%)
  matrix products  22.2 us (8%)
  other arithmetic  14.1 us (5%)
  local copies, waits for them, and re-layouts  8.1 us (3%)
    pallas_call x1, Pallas kernels, gathered(): pl.pallas_call(functools.partial(gather_kernel, plan), in_specs=[vmem] *...  123 us
    pallas_call x1, Pallas kernels, densities(): pl.pallas_call(functools.partial(transform_kernel, grid, offsets, packed)...  63.2 us
    all_gather x1, blocking collectives, local(): lax.all_gather(weight.reshape(-1), ('band', 'col'), axis=0, tiled=False)  54.2 us
    dot_general x1, matrix products, local(): lax.dot_general(both, cols.reshape(depth, -1), (((0,), (0,)), ((), ())),...  22.2 us

profile of v2, /device:TPU:8, one launch (start us, length us, event | category | flops | bytes accessed | tf_op | source)
XLA Modules:
  0.0 284.5 jit_solution(931705904894462778)
XLA Ops:
  0.0 0.8 fusion.14
  0.8 0.1 reshape.82
  0.9 54.2 %all-gather = f32[32,1,16]{2,1,0:T(1,128)S(1)} all-gather(f32[1,1,16]{2,1,0:T(1,128)S(1)} %reshape.82), channel_id=1, replica_groups=mesh['band'=16,'col'=2] {'band','col'}, dimensions={0}, use_global_device_ids=true | all-gather | bytes 2112 | tf_op jit(solution)/shard_map/all_gather | solution.py:432
  55.1 0.5 broadcast.99
  55.6 0.7 reduce.3
  56.3 0.1 mul.25
  56.4 1.6 fusion.11
  58.0 0.1 mul.26
  58.1 0.2 mul.27
  58.3 63.2 %transform.1.field_ref = f32[32,32,640]{2,1,0:T(8,128)} custom-call(bf16[4,64,64,128]{3,2,1,0:T(8,128)(2,1)} %val_ref.1, bf16[4,64,64,128]{3,2,1,0:T(8,128)(2,1)} %cond_ref.1, bf16[256,256]{1,0:T(8,128)(2,1)} %constant.177.clone.z_ref, bf16[128,256]{1,0:T(8,128)(2,1)} %constant.178.clone.y_ref, bf16[64,256]{1,0:T(8,128)(2,1)} %constant.179.clone.x_ref), custom_call_target="tpu_custom_call" | custom-call | tf_op jit(solution)/shard_map/transform/pallas_call | solution.py:342
  121.5 122.7 %pick_and_gather.1 = (bf16[16,2,32,5120]{3,2,1,0:T(8,128)(2,1)}, bf16[16,2,32,640]{3,2,1,0:T(8,128)(2,1)}) custom-call(f32[32,32,640]{2,1,0:T(8,128)} %transform.1.field_ref, s32[1,10240]{1,0:T(1,128)} %bitcast.18, s32[1,10240]{1,0:T(1,128)} %bitcast.17), custom_call_target="tpu_custom_call" | custom-call | tf_op jit(solution)/shard_map/pick_and_gather/pallas_call | solution.py:386
  244.1 2.7 fusion
  246.9 3.1 %reshape.81 = f32[512,2,640]{2,1,0:T(2,128)S(1)} reshape(bf16[16,2,32,640]{3,2,1,0:T(8,128)(2,1)} %get-tuple-element.7) | data formatting | bytes 3932160 | tf_op jit(solution)/shard_map/convert_element_type | solution.py:436
  249.9 1.0 multiply_convert_fusion
  251.0 2.4 fusion.15
  253.3 3.0 %pad_maximum_fusion = bf16[512,2,640]{2,1,0:T(2,128)(2,1)S(1)} fusion(bf16[512,1,640]{2,1,0:T(2,128)(2,1)S(1)} %get-tuple-element.10, bf16[512,1,640]{2,1,0:T(2,128)(2,1)S(1)} %get-tuple-element.9), kind=kLoop, calls=%fused_computation.5 | loop fusion | flops 2621440 | bytes 2621440 | tf_op jit(solution)/shard_map/stack | solution.py:438
  256.3 1.4 reshape.78
  257.7 1.9 maximum_bitcast_fusion
  259.6 2.7 copy.13
  262.3 22.2 %fusion.16 = f32[2,640,5120]{2,1,0:T(8,128)} fusion(bf16[2,640,1024]{2,1,0:T(8,128)(2,1)} %bitcast.16, bf16[1024,5120,1]{1,0,2:T(8,128)(2,1)} %bitcast.19), kind=kOutput, calls=%fused_computation.44 | convolution fusion | flops 13421772800 | bytes 39321600 | tf_op jit(solution)/shard_map/dot_general | solution.py:440

commit v3 on v2

--- a/solution.py
+++ b/solution.py
@@ -100,7 +100,7 @@
             mid[side, pl.ds(start, 4 * PAD), :] = found[:, side * half : (side + 1) * half]
         return carry
 
-    lax.fori_loop(0, grid // 2, planes, 0)
+    lax.fori_loop(0, grid // 2, planes, 0, unroll=4)
     cols[...] = jnp.zeros_like(cols)
     count = len(offsets) - 1
     for first in range(0, count, 2):
@@ -140,7 +140,7 @@
 
 
 def gather_kernel(
-    plan, field_ref, col_ref, sel_ref, all_ref, row_ref, held, stage,
+    plan, field_ref, col_ref, sel_ref, weight_ref, all_ref, row_ref, scale_ref, held, stage,
     x_send, x_recv, x_local, send, recv, r_send, r_recv, r_local,
 ):
     count, rows, packed, n_band, n_col, chunks, width, tile, share, window = plan
@@ -181,17 +181,26 @@
     known = (z > 0).astype(jnp.int32) + (z < n_z - 1).astype(jnp.int32) + 1 + n_col
     pl.semaphore_wait(barrier, known)
 
-    held[...] = field_ref[0:count].reshape(count * rows, packed).astype(jnp.bfloat16)
-
     def lanes(j):
         return pl.ds(pl.multiple_of(j * width, 128), width)
 
     def block(slot, j):
         return all_ref.at[slot, :, :, lanes(j)]
 
-    def relay(slot, j, kind, target):
+    def relay(act, slot, j, kind, target):
         view = block(slot, j)
-        return remote(view, view, send.at[j, kind, slot], recv.at[j, slot], band=target)
+        copy = remote(view, view, send.at[j, kind, slot], recv.at[j, slot], band=target)
+        getattr(copy, act)()
+
+        @pl.when(j == 0)
+        def _():
+            view = scale_ref.at[slot]
+            getattr(
+                remote(
+                    view, view, send.at[chunks, kind, slot], recv.at[chunks, slot], band=target
+                ),
+                act,
+            )()
 
     def staged(j, owner):
         return stage.at[:, pl.ds(pl.multiple_of(owner * span + j * width, 128), width)]
@@ -206,6 +215,18 @@
             col=peer,
         )
 
+    def across_scale(p):
+        return remote(
+            weight_ref,
+            scale_ref.at[me, my_col],
+            x_send.at[chunks, p],
+            x_recv.at[chunks, p],
+            col=(my_col + p) % n_col,
+        )
+
+    def own_scale():
+        return pltpu.make_async_copy(weight_ref, scale_ref.at[me, my_col], x_local.at[chunks])
+
     def own(j):
         return pltpu.make_async_copy(
             staged(j, my_col), all_ref.at[me, my_col, :, lanes(j)], x_local.at[j]
@@ -232,6 +253,12 @@
             own(j).wait()
             for p in range(1, n_col):
                 across(j, p).wait_recv()
+
+            @pl.when(j == 0)
+            def _():
+                for p in range(1, n_col):
+                    across_scale(p).wait_recv()
+
         for step in (1, -1):
             source = z - step * h
             slot = source * 4 + y * 2 + core
@@ -239,15 +266,15 @@
             @pl.when(inside(source))
             def _():
                 if h > 0 and act == "start":
-                    relay(slot, j, 2, y_peer).wait_recv()
+                    relay("wait_recv", slot, j, 2, y_peer)
 
                 @pl.when(inside(z + step))
                 def _():
-                    getattr(relay(slot, j, 0 if step == 1 else 1, me + 4 * step), act)()
+                    relay(act, slot, j, 0 if step == 1 else 1, me + 4 * step)
 
                 if h > 0 or step == 1:
-                    getattr(relay(slot, j, 2, y_peer), act)()
-                    getattr(relay(slot, j, 3, core_peer), act)()
+                    relay(act, slot, j, 2, y_peer)
+                    relay(act, slot, j, 3, core_peer)
 
     def along_y(j, h, act):
         for step in (1, -1) if h > 0 else (1,):
@@ -256,10 +283,9 @@
 
             @pl.when(inside(source))
             def _():
-                copy = relay(slot, j, 3, core_peer)
                 if act == "start":
-                    copy.wait_recv()
-                getattr(copy, act)()
+                    relay("wait_recv", slot, j, 3, core_peer)
+                relay(act, slot, j, 3, core_peer)
 
     per_col = n_band // n_col
     owner = me // per_col
@@ -284,7 +310,7 @@
     def finish(j):
         for other in range(2 * n_z):
             slot = other * 2 + 1 - core
-            relay(slot, j, 3, core_peer).wait_recv()
+            relay("wait_recv", slot, j, 3, core_peer)
         for i in range(window // 128):
 
             @pl.when((owner == my_col) & ((base + 128 * i) // width == j))
@@ -292,6 +318,12 @@
                 row_local(i).start()
                 for p in range(1, n_col):
                     row_copy(i, p).start()
+
+    own_scale().start()
+    for p in range(1, n_col):
+        across_scale(p).start()
+    own_scale().wait()
+    held[...] = field_ref[0:count].reshape(count * rows, packed).astype(jnp.bfloat16)
 
     def tick(t, carry):
         def at(lag, act):
@@ -316,6 +348,8 @@
         return carry
 
     lax.fori_loop(0, chunks, settle, 0)
+    for p in range(1, n_col):
+        across_scale(p).wait_send()
     for i in range(window // 128):
 
         @pl.when(owner == my_col)
@@ -370,7 +404,7 @@
     return field, col[None], (z_comp + reach)[None], count, packed
 
 
-def gathered(field, col, sel, count, packed):
+def gathered(weight, field, col, sel, count, packed):
     features, npw = field.shape[1], col.shape[1]
     n_band, n_col = lax.axis_size("band"), lax.axis_size("col")
     chunks = 5
@@ -383,22 +417,23 @@
     vmem = pl.BlockSpec(memory_space=pltpu.VMEM)
     dma = pltpu.SemaphoreType.DMA
     pieces = window // 128
-    cols, rows = pl.pallas_call(
+    cols, rows, scale = pl.pallas_call(
         functools.partial(gather_kernel, plan),
-        in_specs=[vmem] * 3,
-        out_specs=[pl.BlockSpec(memory_space=pl.ANY)] * 2,
+        in_specs=[vmem] * 4,
+        out_specs=[pl.BlockSpec(memory_space=pl.ANY)] * 3,
         out_shape=[
             jax.ShapeDtypeStruct((n_band, n_col, features, chunks * width), jnp.bfloat16),
             jax.ShapeDtypeStruct((n_band, n_col, features, window), jnp.bfloat16),
+            jax.ShapeDtypeStruct((n_band, n_col, 8, 128), jnp.float32),
         ],
         scratch_shapes=[
             pltpu.VMEM((count * features, packed), jnp.bfloat16),
             pltpu.VMEM((features, npw), jnp.bfloat16),
-            dma((chunks, n_col)),
-            dma((chunks, n_col)),
-            dma((chunks,)),
-            dma((chunks, 4, n_band)),
-            dma((chunks, n_band)),
+            dma((chunks + 1, n_col)),
+            dma((chunks + 1, n_col)),
+            dma((chunks + 1,)),
+            dma((chunks + 1, 4, n_band)),
+            dma((chunks + 1, n_band)),
             dma((pieces, n_col)),
             dma((pieces,)),
             dma((pieces,)),
@@ -407,11 +442,11 @@
             vmem_limit_bytes=VMEM, collective_id=0, has_side_effects=True
         ),
         name="pick_and_gather",
-    )(field, col, sel)
+    )(field, col, sel, jnp.zeros((8, 128), jnp.float32).at[0, :features].set(weight))
     if share % 128:
         start = lax.axis_index("band") % (n_band // n_col) * share % 128
         rows = lax.dynamic_slice_in_dim(rows, start, share, axis=3)
-    return cols, rows
+    return cols, rows, scale[:, :, 0, :features].reshape(1, -1)
 
 
 def pair_weights(energy_valence, energy_conduction, occ_valence, occ_conduction):
@@ -425,25 +460,48 @@
     )
 
 
+def contract_kernel(share, row_ref, scale_ref, col_ref, out_ref, left):
+    @pl.when(pl.program_id(0) == 0)
+    def _():
+        rows = (row_ref[...].astype(jnp.float32).T * scale_ref[...]).astype(jnp.bfloat16)
+        left[0:share] = rows
+        wide = rows.astype(jnp.float32)
+        depth = wide.shape[1]
+        even = lax.broadcasted_iota(jnp.int32, wide.shape, 1) % 2 == 0
+        turned = jnp.where(even, pltpu.roll(wide, depth - 1, 1), -pltpu.roll(wide, 1, 1))
+        left[share : 2 * share] = turned.astype(jnp.bfloat16)
+
+    for part in range(2):
+        out_ref[part] = jnp.dot(
+            left[part * share : (part + 1) * share],
+            col_ref[...],
+            preferred_element_type=jnp.float32,
+        )
+
+
 def local(
     valence, conduction, energy_valence, energy_conduction, occ_valence, occ_conduction, gvec_index
 ):
     weight = pair_weights(energy_valence, energy_conduction, occ_valence, occ_conduction)
-    weight = lax.all_gather(weight.reshape(-1), ("band", "col"), axis=0, tiled=False)
-    cols, rows = gathered(*densities(valence, conduction, gvec_index))
+    weight = jnp.repeat(weight.reshape(-1), 2)
+    cols, rows, scale = gathered(weight, *densities(valence, conduction, gvec_index))
     n_band, n_col, features, share = rows.shape
-    depth = n_band * n_col * features
-    rows = rows.reshape(depth // 2, 2, share).astype(jnp.float32)
-    rows = (weight.reshape(-1)[:, None, None] * rows).astype(jnp.bfloat16)
-    turned = jnp.stack([rows[:, 1], -rows[:, 0]], axis=1)
-    both = jnp.concatenate([rows.reshape(depth, share), turned.reshape(depth, share)], axis=1)
-    tile = lax.dot_general(
-        both,
-        cols.reshape(depth, -1),
-        (((0,), (0,)), ((), ())),
-        preferred_element_type=jnp.float32,
-    )
-    return tile.reshape(2, share, cols.shape[3])
+    depth, span = n_band * n_col * features, cols.shape[3]
+    tile = 512 if span % 512 == 0 else 256
+    return pl.pallas_call(
+        functools.partial(contract_kernel, share),
+        grid=(span // tile,),
+        in_specs=[
+            pl.BlockSpec((depth, share), lambda h: (0, 0)),
+            pl.BlockSpec((1, depth), lambda h: (0, 0)),
+            pl.BlockSpec((depth, tile), lambda h: (0, h)),
+        ],
+        out_specs=pl.BlockSpec((2, share, tile), lambda h: (0, 0, h)),
+        out_shape=jax.ShapeDtypeStruct((2, share, span), jnp.float32),
+        scratch_shapes=[pltpu.VMEM((2 * share, depth), jnp.bfloat16)],
+        compiler_params=pltpu.CompilerParams(vmem_limit_bytes=VMEM),
+        name="contract",
+    )(rows.reshape(depth, share), scale, cols.reshape(depth, span))
 
 
 def solution(mesh):

time: 290 us -> 191 us (0.66)
  the two profiles are of different devices: /device:TPU:8 before, /device:TPU:31 now
where the time goes in v3:
time: 191 us; the launch traced here: 190 us
  Pallas kernels  186 us (97%)
  local copies, waits for them, and re-layouts  2.49 us (1%)
  other arithmetic  2.42 us (1%)
    pallas_call x1, Pallas kernels, gathered(): pl.pallas_call(functools.partial(gather_kernel, plan), in_specs=[vmem] *...  119 us
    pallas_call x1, Pallas kernels, densities(): pl.pallas_call(functools.partial(transform_kernel, grid, offsets, packed)...  44.3 us
    pallas_call x1, Pallas kernels, local(): pl.pallas_call(functools.partial(contract_kernel, share), grid=(span // t...  22.2 us

profile of v3, /device:TPU:31, one launch (start us, length us, event | category | flops | bytes accessed | tf_op | source)
XLA Modules:
  0.0 190.4 jit_solution(4870030778464972571)
XLA Ops:
  0.0 0.8 fusion.13
  0.8 0.1 div.42
  0.9 0.1 broadcast_in_dim.150
  0.9 0.1 reshape.54
  1.0 0.6 scatter.4.weight_ref
  1.6 1.6 fusion.10
  3.3 44.3 %transform.1.field_ref = f32[32,32,640]{2,1,0:T(8,128)} custom-call(bf16[4,64,64,128]{3,2,1,0:T(8,128)(2,1)} %val_ref.1, bf16[4,64,64,128]{3,2,1,0:T(8,128)(2,1)} %cond_ref.1, bf16[256,256]{1,0:T(8,128)(2,1)} %constant.204.clone.z_ref, bf16[128,256]{1,0:T(8,128)(2,1)} %constant.205.clone.y_ref, bf16[64,256]{1,0:T(8,128)(2,1)} %constant.206.clone.x_ref), custom_call_target="tpu_custom_call" | custom-call | tf_op jit(solution)/shard_map/transform/pallas_call | solution.py:376
  47.6 119.1 %pick_and_gather.1 = (bf16[16,2,32,5120]{3,2,1,0:T(8,128)(2,1)}, bf16[16,2,32,640]{3,2,1,0:T(8,128)(2,1)}, f32[16,2,8,128]{3,2,1,0:T(8,128)}) custom-call(f32[32,32,640]{2,1,0:T(8,128)} %transform.1.field_ref, s32[1,10240]{1,0:T(1,128)} %bitcast.7, s32[1,10240]{1,0:T(1,128)} %bitcast.6, f32[8,128]{1,0:T(8,128)} %scatter.4.weight_ref), custom_call_target="tpu_custom_call" | custom-call | tf_op jit(solution)/shard_map/pick_and_gather/pallas_call | solution.py:420
  166.6 1.0 slice_reduce_fusion
  167.6 0.7 reshape_squeeze.3.scale_ref
  168.3 22.2 %contract.1 = f32[2,640,5120]{2,1,0:T(8,128)} custom-call(bf16[1024,640]{1,0:T(8,128)(2,1)} %bitcast.5, f32[1,1024]{1,0:T(1,128)} %reshape_squeeze.3.scale_ref, bf16[1024,5120]{1,0:T(8,128)(2,1)} %bitcast.4), custom_call_target="tpu_custom_call" | custom-call | tf_op jit(solution)/shard_map/contract/pallas_call | solution.py:491

commit v4 on v3

--- a/solution.py
+++ b/solution.py
@@ -143,14 +143,14 @@
     plan, field_ref, col_ref, sel_ref, weight_ref, all_ref, row_ref, scale_ref, held, stage,
     x_send, x_recv, x_local, send, recv, r_send, r_recv, r_local,
 ):
-    count, rows, packed, n_band, n_col, chunks, width, tile, share, window = plan
+    count, rows, packed, n_band, n_col, chunks, groups, share, window = plan
     n_z = n_band // 4
     me = lax.axis_index("band")
     my_col = lax.axis_index("col")
     z, y, core = me // 4, me // 2 % 2, me % 2
     y_peer = z * 4 + (1 - y) * 2 + core
     core_peer = z * 4 + y * 2 + 1 - core
-    span = chunks * width
+    group = chunks * 128
 
     def remote(src, dst, send_sem, recv_sem, **target):
         return pltpu.make_async_remote_copy(
@@ -182,10 +182,10 @@
     pl.semaphore_wait(barrier, known)
 
     def lanes(j):
-        return pl.ds(pl.multiple_of(j * width, 128), width)
+        return pl.ds(pl.multiple_of(j * 128, 128), 128)
 
     def block(slot, j):
-        return all_ref.at[slot, :, :, lanes(j)]
+        return all_ref.at[slot, :, :, :, lanes(j)]
 
     def relay(act, slot, j, kind, target):
         view = block(slot, j)
@@ -203,13 +203,13 @@
             )()
 
     def staged(j, owner):
-        return stage.at[:, pl.ds(pl.multiple_of(owner * span + j * width, 128), width)]
+        return stage.at[j, owner]
 
     def across(j, p):
         peer = (my_col + p) % n_col
         return remote(
             staged(j, peer),
-            all_ref.at[me, my_col, :, lanes(j)],
+            all_ref.at[me, my_col, :, :, lanes(j)],
             x_send.at[j, p],
             x_recv.at[j, p],
             col=peer,
@@ -229,21 +229,22 @@
 
     def own(j):
         return pltpu.make_async_copy(
-            staged(j, my_col), all_ref.at[me, my_col, :, lanes(j)], x_local.at[j]
+            staged(j, my_col), all_ref.at[me, my_col, :, :, lanes(j)], x_local.at[j]
         )
 
     def pick(j):
-        per = width // tile
+        pieces = min(4, groups)
 
         def body(i, carry):
-            start = pl.multiple_of((i // per) * span + j * width + (i % per) * tile, 128)
-            where = pl.ds(start, tile)
-            stage[:, where] = pick_tile(
-                count, rows, packed, held, col_ref[:, where], sel_ref[:, where]
-            )
+            first = i * pieces
+            start = (j * n_col * groups + first) * 128
+            where = pl.ds(pl.multiple_of(start, 128), pieces * 128)
+            found = pick_tile(count, rows, packed, held, col_ref[:, where], sel_ref[:, where])
+            for k in range(pieces):
+                stage[j, first // groups, first % groups + k] = found[:, k * 128 : (k + 1) * 128]
             return carry
 
-        lax.fori_loop(0, n_col * per, body, 0)
+        lax.fori_loop(0, n_col * groups // pieces, body, 0)
         own(j).start()
         for p in range(1, n_col):
             across(j, p).start()
@@ -290,10 +291,11 @@
     per_col = n_band // n_col
     owner = me // per_col
     base = me % per_col * share // 128 * 128
+    home, first_piece = base // group, base % group // 128
 
     def row_copy(i, p):
         return remote(
-            all_ref.at[:, :, :, pl.ds(pl.multiple_of(base + 128 * i, 128), 128)],
+            all_ref.at[:, :, home, :, lanes(first_piece + i)],
             row_ref.at[:, :, :, pl.ds(128 * i, 128)],
             r_send.at[i, p],
             r_recv.at[i],
@@ -302,7 +304,7 @@
 
     def row_local(i):
         return pltpu.make_async_copy(
-            all_ref.at[:, :, :, pl.ds(pl.multiple_of(base + 128 * i, 128), 128)],
+            all_ref.at[:, :, home, :, lanes(first_piece + i)],
             row_ref.at[:, :, :, pl.ds(128 * i, 128)],
             r_local.at[i],
         )
@@ -313,7 +315,7 @@
             relay("wait_recv", slot, j, 3, core_peer)
         for i in range(window // 128):
 
-            @pl.when((owner == my_col) & ((base + 128 * i) // width == j))
+            @pl.when((owner == my_col) & (first_piece + i == j))
             def _():
                 row_local(i).start()
                 for p in range(1, n_col):
@@ -408,12 +410,18 @@
     features, npw = field.shape[1], col.shape[1]
     n_band, n_col = lax.axis_size("band"), lax.axis_size("col")
     chunks = 5
-    width = npw // n_col // chunks
-    tile = min(512, width)
+    groups = npw // n_col // (chunks * 128)
     share = npw // n_band
     window = -(-share // 128) * 128
     assert window >= share + max(share * r % 128 for r in range(n_band // n_col))
-    plan = (count, features, packed, n_band, n_col, chunks, width, tile, share, window)
+    for r in range(n_band // n_col):
+        assert share * r % (chunks * 128) // 128 * 128 + window <= chunks * 128
+    plan = (count, features, packed, n_band, n_col, chunks, groups, share, window)
+
+    def reorder(values):
+        values = values.reshape(n_col, groups, chunks, 128)
+        return jnp.transpose(values, (2, 0, 1, 3)).reshape(1, npw)
+
     vmem = pl.BlockSpec(memory_space=pltpu.VMEM)
     dma = pltpu.SemaphoreType.DMA
     pieces = window // 128
@@ -422,13 +430,15 @@
         in_specs=[vmem] * 4,
         out_specs=[pl.BlockSpec(memory_space=pl.ANY)] * 3,
         out_shape=[
-            jax.ShapeDtypeStruct((n_band, n_col, features, chunks * width), jnp.bfloat16),
+            jax.ShapeDtypeStruct(
+                (n_band, n_col, groups, features, chunks * 128), jnp.bfloat16
+            ),
             jax.ShapeDtypeStruct((n_band, n_col, features, window), jnp.bfloat16),
             jax.ShapeDtypeStruct((n_band, n_col, 8, 128), jnp.float32),
         ],
         scratch_shapes=[
             pltpu.VMEM((count * features, packed), jnp.bfloat16),
-            pltpu.VMEM((features, npw), jnp.bfloat16),
+            pltpu.VMEM((chunks, n_col, groups, features, 128), jnp.bfloat16),
             dma((chunks + 1, n_col)),
             dma((chunks + 1, n_col)),
             dma((chunks + 1,)),
@@ -442,7 +452,7 @@
             vmem_limit_bytes=VMEM, collective_id=0, has_side_effects=True
         ),
         name="pick_and_gather",
-    )(field, col, sel, jnp.zeros((8, 128), jnp.float32).at[0, :features].set(weight))
+    )(field, reorder(col), reorder(sel), jnp.zeros((8, 128), jnp.float32).at[0, :features].set(weight))
     if share % 128:
         start = lax.axis_index("band") % (n_band // n_col) * share % 128
         rows = lax.dynamic_slice_in_dim(rows, start, share, axis=3)
@@ -471,10 +481,14 @@
         turned = jnp.where(even, pltpu.roll(wide, depth - 1, 1), -pltpu.roll(wide, 1, 1))
         left[share : 2 * share] = turned.astype(jnp.bfloat16)
 
+    cols = col_ref[...]
+    if cols.shape[3] % 16:
+        cols = cols.astype(jnp.float32)
+    cols = cols.reshape(left.shape[1], cols.shape[4]).astype(jnp.bfloat16)
     for part in range(2):
         out_ref[part] = jnp.dot(
             left[part * share : (part + 1) * share],
-            col_ref[...],
+            cols,
             preferred_element_type=jnp.float32,
         )
 
@@ -486,22 +500,21 @@
     weight = jnp.repeat(weight.reshape(-1), 2)
     cols, rows, scale = gathered(weight, *densities(valence, conduction, gvec_index))
     n_band, n_col, features, share = rows.shape
-    depth, span = n_band * n_col * features, cols.shape[3]
-    tile = 512 if span % 512 == 0 else 256
+    depth, groups, tile = n_band * n_col * features, cols.shape[2], cols.shape[4]
     return pl.pallas_call(
         functools.partial(contract_kernel, share),
-        grid=(span // tile,),
+        grid=(groups,),
         in_specs=[
             pl.BlockSpec((depth, share), lambda h: (0, 0)),
             pl.BlockSpec((1, depth), lambda h: (0, 0)),
-            pl.BlockSpec((depth, tile), lambda h: (0, h)),
+            pl.BlockSpec((n_band, n_col, 1, features, tile), lambda h: (0, 0, h, 0, 0)),
         ],
         out_specs=pl.BlockSpec((2, share, tile), lambda h: (0, 0, h)),
-        out_shape=jax.ShapeDtypeStruct((2, share, span), jnp.float32),
+        out_shape=jax.ShapeDtypeStruct((2, share, groups * tile), jnp.float32),
         scratch_shapes=[pltpu.VMEM((2 * share, depth), jnp.bfloat16)],
         compiler_params=pltpu.CompilerParams(vmem_limit_bytes=VMEM),
         name="contract",
-    )(rows.reshape(depth, share), scale, cols.reshape(depth, span))
+    )(rows.reshape(depth, share), scale, cols)
 
 
 def solution(mesh):

time: 191 us -> 172 us (0.901)
  the two profiles are of different devices: /device:TPU:31 before, /device:TPU:8 now
where the time goes in v4:
time: 172 us
  Pallas kernels  166 us (97%)
  local copies, waits for them, and re-layouts  3.75 us (2%)
  other arithmetic  1.8 us (1%)
    pallas_call x1, Pallas kernels, gathered(): pl.pallas_call(functools.partial(gather_kernel, plan), in_specs=[vmem] *...  99 us
    pallas_call x1, Pallas kernels, densities(): pl.pallas_call(functools.partial(transform_kernel, grid, offsets, packed)...  44.3 us
    pallas_call x1, Pallas kernels, local(): pl.pallas_call(functools.partial(contract_kernel, share), grid=(groups,),...  22.9 us

profile of v4, /device:TPU:8, one launch (start us, length us, event | category | flops | bytes accessed | tf_op | source)
XLA Modules:
  0.0 171.8 jit_solution(14596867157318089312)
XLA Ops:
  0.0 0.8 fusion.13
  0.8 0.1 div.42
  0.9 0.1 broadcast_in_dim.142
  0.9 0.1 reshape.59
  1.0 0.6 scatter.4.weight_ref
  1.6 1.0 fusion.10
  2.7 0.6 copy.12
  3.3 0.6 copy.11
  3.9 44.3 %transform.1.field_ref = f32[32,32,640]{2,1,0:T(8,128)} custom-call(bf16[4,64,64,128]{3,2,1,0:T(8,128)(2,1)} %val_ref.1, bf16[4,64,64,128]{3,2,1,0:T(8,128)(2,1)} %cond_ref.1, bf16[256,256]{1,0:T(8,128)(2,1)} %constant.204.clone.z_ref, bf16[128,256]{1,0:T(8,128)(2,1)} %constant.205.clone.y_ref, bf16[64,256]{1,0:T(8,128)(2,1)} %constant.206.clone.x_ref), custom_call_target="tpu_custom_call" | custom-call | tf_op jit(solution)/shard_map/transform/pallas_call | solution.py:378
  48.2 99.0 %pick_and_gather.1 = (bf16[16,2,8,32,640]{4,3,2,1,0:T(8,128)(2,1)}, bf16[16,2,32,640]{3,2,1,0:T(8,128)(2,1)}, f32[16,2,8,128]{3,2,1,0:T(8,128)}) custom-call(f32[32,32,640]{2,1,0:T(8,128)} %transform.1.field_ref, s32[1,10240]{1,0:T(1,128)} %bitcast.9, s32[1,10240]{1,0:T(1,128)} %bitcast.8, f32[8,128]{1,0:T(8,128)} %scatter.4.weight_ref), custom_call_target="tpu_custom_call" | custom-call | tf_op jit(solution)/shard_map/pick_and_gather/pallas_call | solution.py:428
  147.3 1.0 slice_reduce_fusion
  148.2 0.7 reshape_squeeze.3.scale_ref
  148.9 22.9 %contract.1 = f32[2,640,5120]{2,1,0:T(8,128)} custom-call(bf16[1024,640]{1,0:T(8,128)(2,1)} %bitcast.5, f32[1,1024]{1,0:T(1,128)} %reshape_squeeze.3.scale_ref, bf16[16,2,8,32,640]{4,3,2,1,0:T(8,128)(2,1)} %get-tuple-element.22.col_ref), custom_call_target="tpu_custom_call" | custom-call | tf_op jit(solution)/shard_map/contract/pallas_call | solution.py:504
  (2 shorter events, 0.0 us)

commit v5 on v4

--- a/solution.py
+++ b/solution.py
@@ -100,7 +100,7 @@
             mid[side, pl.ds(start, 4 * PAD), :] = found[:, side * half : (side + 1) * half]
         return carry
 
-    lax.fori_loop(0, grid // 2, planes, 0, unroll=4)
+    lax.fori_loop(0, grid // 2, planes, 0, unroll=8)
     cols[...] = jnp.zeros_like(cols)
     count = len(offsets) - 1
     for first in range(0, count, 2):
@@ -244,7 +244,7 @@
                 stage[j, first // groups, first % groups + k] = found[:, k * 128 : (k + 1) * 128]
             return carry
 
-        lax.fori_loop(0, n_col * groups // pieces, body, 0)
+        lax.fori_loop(0, n_col * groups // pieces, body, 0, unroll=2)
         own(j).start()
         for p in range(1, n_col):
             across(j, p).start()
@@ -333,10 +333,11 @@
             pl.when((j >= 0) & (j < chunks))(lambda: act(j))
 
         at(0, pick)
+        for h in range(n_z):
+            at(1 + h, lambda j: along_z(j, h, "start"))
+        for h in range(n_z):
+            at(2 + h, lambda j: along_y(j, h, "start"))
         at(n_z + 2, finish)
-        for h in range(n_z - 1, -1, -1):
-            at(2 + h, lambda j: along_y(j, h, "start"))
-            at(1 + h, lambda j: along_z(j, h, "start"))
         return carry
 
     lax.fori_loop(0, chunks + n_z + 2, tick, 0)

time: 172 us -> 176 us (1.023)
  Pallas kernels: 166 us -> 170 us
    pallas_call x1, Pallas kernels: 99 us -> 106 us  [gathered(): pl.pallas_call(functools.partial(gather_kernel, plan), in_specs=[vmem] *...]
    pallas_call x1, Pallas kernels: 44.3 us -> 40.9 us  [densities(): pl.pallas_call(functools.partial(transform_kernel, grid, offsets, packed)...]
where the time goes in v5:
time: 176 us; the launch traced here: 175 us
  Pallas kernels  170 us (97%)
  local copies, waits for them, and re-layouts  3.75 us (2%)
  other arithmetic  1.8 us (1%)
    pallas_call x1, Pallas kernels, gathered(): pl.pallas_call(functools.partial(gather_kernel, plan), in_specs=[vmem] *...  106 us
    pallas_call x1, Pallas kernels, densities(): pl.pallas_call(functools.partial(transform_kernel, grid, offsets, packed)...  40.9 us
    pallas_call x1, Pallas kernels, local(): pl.pallas_call(functools.partial(contract_kernel, share), grid=(groups,),...  22.9 us

profile of v5, /device:TPU:8, one launch (start us, length us, event | category | flops | bytes accessed | tf_op | source)
XLA Modules:
  0.0 175.3 jit_solution(17190032860108973042)
XLA Ops:
  0.0 0.8 fusion.13
  0.8 0.1 div.42
  0.9 0.1 broadcast_in_dim.142
  0.9 0.1 reshape.59
  1.0 0.6 scatter.4.weight_ref
  1.6 1.0 fusion.10
  2.7 0.6 copy.12
  3.3 0.6 copy.11
  3.9 40.9 %transform.1.field_ref = f32[32,32,640]{2,1,0:T(8,128)} custom-call(bf16[4,64,64,128]{3,2,1,0:T(8,128)(2,1)} %val_ref.1, bf16[4,64,64,128]{3,2,1,0:T(8,128)(2,1)} %cond_ref.1, bf16[256,256]{1,0:T(8,128)(2,1)} %constant.204.clone.z_ref, bf16[128,256]{1,0:T(8,128)(2,1)} %constant.205.clone.y_ref, bf16[64,256]{1,0:T(8,128)(2,1)} %constant.206.clone.x_ref), custom_call_target="tpu_custom_call" | custom-call | tf_op jit(solution)/shard_map/transform/pallas_call | solution.py:379
  44.8 106.0 %pick_and_gather.1 = (bf16[16,2,8,32,640]{4,3,2,1,0:T(8,128)(2,1)}, bf16[16,2,32,640]{3,2,1,0:T(8,128)(2,1)}, f32[16,2,8,128]{3,2,1,0:T(8,128)}) custom-call(f32[32,32,640]{2,1,0:T(8,128)} %transform.1.field_ref, s32[1,10240]{1,0:T(1,128)} %bitcast.9, s32[1,10240]{1,0:T(1,128)} %bitcast.8, f32[8,128]{1,0:T(8,128)} %scatter.4.weight_ref), custom_call_target="tpu_custom_call" | custom-call | tf_op jit(solution)/shard_map/pick_and_gather/pallas_call | solution.py:429
  150.8 1.0 slice_reduce_fusion
  151.8 0.7 reshape_squeeze.3.scale_ref
  152.4 22.9 %contract.1 = f32[2,640,5120]{2,1,0:T(8,128)} custom-call(bf16[1024,640]{1,0:T(8,128)(2,1)} %bitcast.5, f32[1,1024]{1,0:T(1,128)} %reshape_squeeze.3.scale_ref, bf16[16,2,8,32,640]{4,3,2,1,0:T(8,128)(2,1)} %get-tuple-element.22.col_ref), custom_call_target="tpu_custom_call" | custom-call | tf_op jit(solution)/shard_map/contract/pallas_call | solution.py:505
  (2 shorter events, 0.0 us)
